TPU v7x, 256 devices: a whole 4x4x8 slice. The times are simulated.
256 devices in a mesh: node: 32 (over x, y, core), local: 8 (over z).
Axes of the slice: x: 4, y: 4, z: 8, core: 2. Of those that a mesh axis runs over, the one named last changes fastest.
Arguments:
- tokens: bfloat16 [4096, 7168], P('node', 'local'), may hold values from -6 to 6
- w_gate: bfloat16 [32, 7168, 1024], P('node', 'local'), may hold values from -0.0625 to 0.0625
- w_up: bfloat16 [32, 7168, 1024], P('node', 'local'), may hold values from -0.0625 to 0.0625
- w_down: bfloat16 [32, 1024, 7168], P('node', None, 'local'), may hold values from -0.1875 to 0.1875
- expert_ids: int32 [4096, 8], P('node'), may hold values from 0 to 31, all different within a row; in each aligned block of 128 rows (0 to 127, 128 to 255, ...) at most 64 rows name the same one
- gate_weights: bfloat16 [4096, 8], P('node'), may hold values from 0.099609375 to 0.59765625
Outputs:
- moe_out: bfloat16 [4096, 7168], P('node', 'local')
Inputs may be any that keep to these rules, and one draw needn't show every extreme that they name: `expert_ids`: each row names 8 different experts. Among the 128 rows of one node no expert is named by more than 64 rows, and in every draw some expert is named by exactly 64 rows of some node.
All inputs are finite; a program needn't handle non-finite values.
Results may differ from a plain program's by a relative error of at most 0.029.
Values may be sent and summed in bfloat16 or wider, within the bound.
A program may use at most 64 MiB of HBM per device.

v0:
```python
import jax
import jax.numpy as jnp
from jax import lax
from jax.sharding import PartitionSpec as P


def slot_tables(expert_ids, gate_weights, node_count, capacity):
    tok_rows, top_count = expert_ids.shape
    expert_iota = jnp.arange(node_count, dtype=jnp.int32)
    member = jnp.zeros((tok_rows, node_count), jnp.int32)
    for position in range(top_count):
        member = member + (expert_ids[:, position][:, None] == expert_iota[None, :]).astype(
            jnp.int32
        )
    before = jnp.cumsum(member, axis=0) - member
    slot_iota = jnp.arange(node_count * capacity, dtype=jnp.int32)
    select = jnp.zeros((tok_rows, node_count * capacity), jnp.float32)
    combine = jnp.zeros((tok_rows, node_count * capacity), jnp.float32)
    for position in range(top_count):
        target = expert_ids[:, position]
        onehot = (target[:, None] == expert_iota[None, :]).astype(jnp.int32)
        placed = target * capacity + jnp.sum(onehot * before, axis=1)
        matches = placed[:, None] == slot_iota[None, :]
        select = select + matches.astype(jnp.float32)
        combine = combine + jnp.where(
            matches, gate_weights[:, position].astype(jnp.float32)[:, None], 0.0
        )
    return (select.astype(jnp.bfloat16), combine.astype(jnp.bfloat16))


def per_device(tokens, w_gate, w_up, w_down, expert_ids, gate_weights):
    node_count = lax.axis_size("node")
    tok_rows, features = tokens.shape
    capacity = min(tok_rows, 2 * tok_rows * expert_ids.shape[1] // node_count)
    select, combine = slot_tables(expert_ids, gate_weights, node_count, capacity)
    outbound = lax.dot_general(
        select, tokens, (((0,), (0,)), ((), ())), preferred_element_type=jnp.float32
    )
    outbound = outbound.astype(jnp.bfloat16).reshape(node_count, capacity, features)
    arrived = lax.all_to_all(outbound, "node", split_axis=0, concat_axis=0, tiled=True)
    row_block = arrived.reshape(node_count * capacity, features)
    gate_mat = w_gate[0]
    up_mat = w_up[0]
    down_mat = w_down[0]
    contract = (((0,), (1,)), ((), ()))
    gate_part = lax.dot_general(gate_mat, row_block, contract, preferred_element_type=jnp.float32)
    up_part = lax.dot_general(up_mat, row_block, contract, preferred_element_type=jnp.float32)
    reduced = lax.psum_scatter(
        jnp.stack([gate_part, up_part], axis=1).astype(jnp.bfloat16),
        "local",
        scatter_dimension=0,
        tiled=True,
    ).astype(jnp.float32)
    activated = (jax.nn.silu(reduced[:, 0]) * reduced[:, 1]).astype(jnp.bfloat16)
    expert_out = lax.dot_general(
        lax.all_gather(activated, "local", axis=0, tiled=True),
        down_mat,
        (((0,), (0,)), ((), ())),
        preferred_element_type=jnp.float32,
    )
    returned = expert_out.astype(jnp.bfloat16).reshape(node_count, capacity, features)
    homeward = lax.all_to_all(returned, "node", split_axis=0, concat_axis=0, tiled=True)
    merged = jnp.dot(
        combine,
        homeward.reshape(node_count * capacity, features),
        preferred_element_type=jnp.float32,
    )
    return merged.astype(jnp.bfloat16)


def solution(mesh):
    placed = (
        P("node", "local"),
        P("node", "local", None),
        P("node", "local", None),
        P("node", None, "local"),
        P("node", None),
        P("node", None),
    )
    return jax.shard_map(
        per_device, mesh=mesh, in_specs=placed, out_specs=P("node", "local"), check_vma=False
    )
```

profile of v0, /device:TPU:1, one launch (start us, length us, event | category | flops | bytes accessed | tf_op | source)
XLA Modules:
  0.0 326.3 jit_solution(5337715470079070059)
XLA Ops:
  6.5 0.0 copy-start
  6.5 0.0 reduce-scatter.4.cloned.1.call-start
  6.5 1.0 slice_bitcast_fusion.8
  7.5 0.2 convert_add_fusion
  7.7 0.2 reduce_window_sum.11
  7.9 0.4 select_reduce_fusion.7
  8.3 1.0 fusion.37
  9.3 3.0 convolution_convert_fusion.1
  12.3 53.7 %all_to_all.10 = bf16[32,64,896]{2,1,0:T(8,128)(2,1)S(1)} all-to-all(bf16[32,64,896]{2,1,0:T(8,128)(2,1)S(1)} %bitcast.132), channel_id=1, replica_groups=mesh['node'=32,'local'=8] {'node'}, dimensions={0} | all-to-all | bytes 7340032 | tf_op jit(solution)/shard_map/all_to_all | solution.py:40
  66.0 0.0 copy-done
  66.0 0.0 copy-start.2
  66.0 4.7 %convert_bitcast_fusion = bf16[1024,1,2048]{0,2,1:T(8,128)(2,1)S(1)} fusion(bf16[2048,896]{1,0:T(8,128)(2,1)S(1)} %bitcast.130, bf16[1,896,1024]{2,1,0:T(8,128)(2,1)S(1)} %copy-done), kind=kOutput, calls=%fused_computation.1 | convolution fusion | flops 3760193536 | bytes 9699328 | tf_op jit(solution)/shard_map/dot_general | solution.py:47
  70.8 0.0 copy-done.2
  70.8 6.0 %convert_bitcast_fusion.1 = bf16[1024,1,2048]{0,2,1:T(8,128)(2,1)} fusion(bf16[2048,896]{1,0:T(8,128)(2,1)S(1)} %bitcast.131, bf16[1,896,1024]{2,1,0:T(8,128)(2,1)S(1)} %copy-done.2), kind=kOutput, calls=%fused_computation.2 | convolution fusion | flops 3760193536 | bytes 9699328 | tf_op jit(solution)/shard_map/dot_general | solution.py:46
  76.8 6.2 %pad_maximum_fusion = bf16[1024,2,2048]{0,2,1:T(8,128)(2,1)} fusion(bf16[1024,1,2048]{0,2,1:T(8,128)(2,1)S(1)} %convert_bitcast_fusion, bf16[1024,1,2048]{0,2,1:T(8,128)(2,1)} %convert_bitcast_fusion.1), kind=kLoop, calls=%fused_computation | loop fusion | flops 4194304 | bytes 16777216 | tf_op jit(solution)/shard_map/stack | solution.py:49
  82.9 11.5 %copy.9 = bf16[1024,4096]{1,0:T(8,128)(2,1)} copy(bf16[1024,4096]{0,1:T(8,128)(2,1)} %bitcast.127) | data formatting | bytes 16777216
  94.4 0.0 reduce-scatter.4.cloned.1.call-update
  94.4 0.2 all-gather.2.cloned.1.call-start
  94.7 93.7 %reduce-scatter.4.cloned.1.call-done = bf16[128,4096]{1,0:T(8,128)(2,1)} async-done(((bf16[1024,4096]{1,0:T(8,128)(2,1)}), bf16[128,4096]{1,0:T(8,128)(2,1)}) %reduce-scatter.4.cloned.1.call-update) | async-done | bytes 1048592
  188.4 1.6 copy.10
  190.0 0.1 convert_element_type.113
  190.2 1.1 fusion.4
  191.3 0.0 all-gather.2.cloned.1.call-update
  191.3 58.5 %all-gather.2.cloned.1.call-done = bf16[1024,2048]{0,1:T(8,128)(2,1)} async-done(((bf16[128,2048]{0,1:T(8,128)(2,1)}), bf16[1024,2048]{0,1:T(8,128)(2,1)}) %all-gather.2.cloned.1.call-update) | async-done | bytes 4194320 | tf_op jit(solution)/shard_map/all_gather | solution.py:56
  249.7 9.1 %convolution_convert_fusion = bf16[2048,896]{1,0:T(8,128)(2,1)} fusion(bf16[1024,2048]{0,1:T(8,128)(2,1)} %all-gather.2.cloned.1.call-done, bf16[1,1024,896]{2,1,0:T(8,128)(2,1)} %param.9), kind=kOutput, calls=%fused_computation.3 | convolution fusion | flops 3759931392 | bytes 9699328 | tf_op jit(solution)/shard_map/dot_general | solution.py:55
  258.9 0.0 copy-start.1
  258.9 10.3 %all-to-all-start.1 = ((bf16[32,64,896]{2,1,0:T(8,128)(2,1)}), bf16[32,64,896]{2,1,0:T(8,128)(2,1)}, u32[]{:S(2)}, u32[]{:S(2)}) async-start(bf16[32,64,896]{2,1,0:T(8,128)(2,1)} %bitcast.129), calls=%async_computation.1 | async-start | bytes 7340032 | tf_op jit(solution)/shard_map/all_to_all | solution.py:62
  269.2 0.0 copy-done.1
  269.2 46.0 %all-to-all-done.1 = bf16[32,64,896]{2,1,0:T(8,128)(2,1)} async-done(((bf16[32,64,896]{2,1,0:T(8,128)(2,1)}), bf16[32,64,896]{2,1,0:T(8,128)(2,1)}, u32[]{:S(2)}, u32[]{:S(2)}) %all-to-all-start.1) | async-done | bytes 3670048 | tf_op jit(solution)/shard_map/all_to_all | solution.py:62
  315.2 4.3 %convolution_convert_fusion.2 = bf16[128,896]{1,0:T(8,128)(2,1)} fusion(bf16[2048,896]{1,0:T(8,128)(2,1)} %bitcast.44, f32[128]{0:T(128)S(1)} %get-tuple-element.35, s32[128]{0:T(128)S(1)} %get-tuple-element.20, f32[128]{0:T(128)S(1)} %get-tuple-element.36, s32[128]{0:T(128)S(1)} %get-tuple-element.19, f32[128]{0:T(128)S(1)} %get-tuple-element.30, ...), kind=kOutput, calls=%fused_computation.8 | convolution fusion | flops 476168192 | bytes 3907584 | tf_op jit(solution)/shard_map/dot_general | solution.py:63
  (1 shorter events, 0.0 us)
Async XLA Ops:
  6.5 59.5 %copy-start = (bf16[1,896,1024]{2,1,0:T(8,128)(2,1)S(1)}, bf16[1,896,1024]{2,1,0:T(8,128)(2,1)}, u32[]{:S(2)}) copy-start(bf16[1,896,1024]{2,1,0:T(8,128)(2,1)} %param.8) | copy-start | bytes 5505028
  6.5 181.9 %reduce-scatter.4.cloned.1.call-start = ((), (), s32[]{:S(2)}) async-start(), calls=%async_computation.4 | async-start | bytes 9437184
  66.0 4.7 %copy-start.2 = (bf16[1,896,1024]{2,1,0:T(8,128)(2,1)S(1)}, bf16[1,896,1024]{2,1,0:T(8,128)(2,1)}, u32[]{:S(2)}) copy-start(bf16[1,896,1024]{2,1,0:T(8,128)(2,1)} %param.7) | copy-start | bytes 5505028
  94.4 155.3 %all-gather.2.cloned.1.call-start = ((), (), s32[]{:S(2)}) async-start(), calls=%async_computation.3 | async-start | bytes 4718592 | tf_op jit(solution)/shard_map/all_gather | solution.py:56
  258.9 10.3 %copy-start.1 = (bf16[128,8]{0,1:T(8,128)(2,1)S(1)}, bf16[128,8]{0,1:T(8,128)(2,1)}, u32[]{:S(2)}) copy-start(bf16[128,8]{0,1:T(8,128)(2,1)} %param.11) | copy-start | bytes 6148
  258.9 56.3 %all-to-all-start.1 = ((bf16[32,64,896]{2,1,0:T(8,128)(2,1)}), bf16[32,64,896]{2,1,0:T(8,128)(2,1)}, u32[]{:S(2)}, u32[]{:S(2)}) async-start(bf16[32,64,896]{2,1,0:T(8,128)(2,1)} %bitcast.129), calls=%async_computation.1 | async-start | bytes 7340032 | tf_op jit(solution)/shard_map/all_to_all | solution.py:62
Sparse Core Ops, SparseCore 0:
  94.6 93.7 reduce-scatter.3
  191.4 58.2 all-gather.1
where the time goes:
time: 327 us; the launch traced here: 326 us
  waiting for transfers between devices  198 us (61%)
  blocking collectives  53.7 us (16%)
  matrix products  27.2 us (8%)
  local copies, waits for them, and re-layouts  14.1 us (4%)
  between operations  13.5 us (4%)
  starting transfers between devices  10.5 us (3%)
  other arithmetic  9.15 us (3%)
    unnamed x3, waiting for transfers between devices  93.8 us
    all_gather x1, waiting for transfers between devices, per_device(): lax.all_gather(activated, 'local', axis=0, tiled=True)  58.5 us
    all_to_all x1, blocking collectives, per_device(): lax.all_to_all(outbound, 'node', split_axis=0, concat_axis=0, tiled=True)  53.7 us
    all_to_all x1, waiting for transfers between devices, per_device(): lax.all_to_all(returned, 'node', split_axis=0, concat_axis=0, tiled=True)  46 us
    unnamed x8, local copies, waits for them, and re-layouts  13.1 us
    all_to_all x1, starting transfers between devices, per_device(): lax.all_to_all(returned, 'node', split_axis=0, concat_axis=0, tiled=True)  10.3 us
    dot_general x1, matrix products, per_device(): lax.dot_general(lax.all_gather(activated, 'local', axis=0, tiled=True), d...  9.11 us
  transfers between devices with their start and end apart: 3, of which 3 were waited for; matrix products, arithmetic and copies ran while one was open for 0% of the time, Pallas kernels for 0%

commit v1 on v0

v1 whole, which is shorter than its diff:
```python
import functools

import jax
import jax.numpy as jnp
from jax import lax
from jax.experimental import pallas as pl
from jax.experimental.pallas import tpu as pltpu
from jax.sharding import PartitionSpec as P

MESH = pl.DeviceIdType.MESH
F32 = jnp.float32
BF16 = jnp.bfloat16

NODES = 32
RING = 8
TOK = 128
FEAT = 896
HID = 1024
HS = HID // RING
CAP = 64
PER = 4
R = PER * CAP
C = NODES // PER
HALF = R // 2


def relative_slot(expert, node):
    dx = (expert // 8 - node // 8) % 4
    dy = ((expert // 2) % 4 - (node // 2) % 4) % 4
    dc = (expert % 2 - node % 2) % 2
    return (dy * 4 + dx) * 2 + dc


def slot_tables(expert_ids, gate_weights):
    node = lax.axis_index("node")
    slots = relative_slot(expert_ids, node).T
    gates = gate_weights.T.astype(F32)
    top = slots.shape[0]
    member = jnp.zeros((NODES, TOK), jnp.int32)
    iota = jnp.arange(NODES, dtype=jnp.int32)
    for k in range(top):
        member = member + (slots[k][None, :] == iota[:, None]).astype(jnp.int32)
    before = jnp.cumsum(member, axis=1) - member
    rows = jnp.arange(NODES * CAP, dtype=jnp.int32)
    select = jnp.zeros((NODES * CAP, TOK), F32)
    combine = jnp.zeros((TOK, NODES * CAP), F32)
    for k in range(top):
        onehot = (slots[k][None, :] == iota[:, None]).astype(jnp.int32)
        placed = slots[k] * CAP + jnp.sum(onehot * before, axis=0)
        select = select + (rows[:, None] == placed[None, :]).astype(F32)
        combine = combine + jnp.where(
            placed[:, None] == rows[None, :], gates[k][:, None], 0.0
        )
    return select.astype(BF16), combine.astype(BF16)


def kernel(
    sel, comb, tok, wg_hbm, wu_hbm, wd_hbm, out,
    wg, wu, wd, outb, arr, snd, rcv, hid, ret, home, acc,
    wsem, dsend, drecv, rsend, rrecv, zsend, zrecv, asend, arecv,
):
    node = lax.axis_index("node")
    z = lax.axis_index("local")
    x, y, core = node // 8, (node // 2) % 4, node % 2
    zup, zdn = (z + 1) % RING, (z + RING - 1) % RING
    neighbour = (zup, zdn)

    weights = [
        pltpu.make_async_copy(src.at[0], dst, wsem.at[k])
        for k, (src, dst) in enumerate(((wg_hbm, wg), (wu_hbm, wu), (wd_hbm, wd)))
    ]
    for copy in weights:
        copy.start()

    def partner(r, sign):
        q = r // 2
        px = (x + sign * (q % 4) + 4) % 4
        py = (y + sign * (q // 4) + 4) % 4
        return (px * 4 + py) * 2 + (core + r) % 2

    barrier = pltpu.get_barrier_semaphore()

    def greet(r, carry):
        pl.semaphore_signal(barrier, inc=1, device_id=(partner(r, 1), z), device_id_type=MESH)
        return carry

    lax.fori_loop(1, NODES, greet, 0)
    for near in neighbour:
        pl.semaphore_signal(barrier, inc=1, device_id=(node, near), device_id_type=MESH)

    def dispatch(r):
        return pltpu.make_async_remote_copy(
            src_ref=outb.at[r], dst_ref=arr.at[r],
            send_sem=dsend.at[r], recv_sem=drecv.at[r],
            device_id=(partner(r, 1), z), device_id_type=MESH,
        )

    def giveback(r):
        return pltpu.make_async_remote_copy(
            src_ref=ret.at[r], dst_ref=home.at[r],
            send_sem=rsend.at[r], recv_sem=rrecv.at[r],
            device_id=(partner(r, -1), z), device_id_type=MESH,
        )

    def partial(i, d, m):
        return pltpu.make_async_remote_copy(
            src_ref=snd.at[i, d, m], dst_ref=rcv.at[i, d, m],
            send_sem=zsend.at[i, d, m], recv_sem=zrecv.at[i, d, m],
            device_id=(node, neighbour[d]), device_id_type=MESH,
        )

    def gather(i, d, a):
        owner = (z + RING - a) % RING if d == 0 else (z + a) % RING
        block = hid.at[i, owner]
        if a == 3:
            block = block.at[pl.ds(d * HALF, HALF)]
        return pltpu.make_async_remote_copy(
            src_ref=block, dst_ref=block,
            send_sem=asend.at[i, d, a], recv_sem=arecv.at[i, d, a],
            device_id=(node, neighbour[d]), device_id_type=MESH,
        )

    def chosen(i):
        rows = sel[pl.ds(pl.multiple_of(i * R, R), R), :]
        return jnp.dot(rows, tok[...], preferred_element_type=F32).astype(BF16)

    first = chosen(0)
    arr[0] = first[:CAP]
    for j in range(1, PER):
        outb[j] = first[j * CAP : (j + 1) * CAP]
    pl.semaphore_wait(barrier, NODES - 1 + 2)
    for j in range(1, PER):
        dispatch(j).start()

    def send_rows(i, carry):
        picked = chosen(i)
        for j in range(PER):
            outb[i * PER + j] = picked[j * CAP : (j + 1) * CAP]
        for j in range(PER):
            dispatch(i * PER + j).start()
        return carry

    lax.fori_loop(1, C, send_rows, 0)
    acc[...] = jnp.zeros_like(acc)
    for copy in weights:
        copy.wait()

    def sums(i, to):
        rows = arr[pl.ds(i * PER, PER)].reshape(R, FEAT)
        cols = pl.ds(pl.multiple_of(to * HS, HS), HS)
        mat = jnp.concatenate([wg[:, cols], wu[:, cols]], axis=1)
        return jnp.dot(rows, mat, preferred_element_type=F32)

    def at(offset):
        return (z + offset + RING) % RING

    def rs_start(i):
        term = sums(i, at(4))
        snd[i, 0, 0] = term[:, :HS].astype(BF16)
        snd[i, 1, 0] = term[:, HS:].astype(BF16)
        partial(i, 0, 0).start()
        partial(i, 1, 0).start()

    def rs_step(i, s):
        terms = (sums(i, at(4 - s)), sums(i, at(s - 4)))
        for part in range(2):
            for d in range(2):
                term = terms[d][:, part * HS : (part + 1) * HS]
                if s == 1:
                    if part == d:
                        partial(i, d, 0).wait_recv()
                        term = term + rcv[i, d, 0].astype(F32)
                else:
                    m = 2 * s - 3 + part
                    partial(i, d, m).wait_recv()
                    term = term + rcv[i, d, m].astype(F32)
                m = 2 * s - 1 + part
                snd[i, d, m] = term.astype(BF16)
                partial(i, d, m).start()

    def finish_sums(i):
        term = sums(i, z)
        total = []
        for part in range(2):
            value = term[:, part * HS : (part + 1) * HS]
            for d in range(2):
                partial(i, d, 5 + part).wait_recv()
                value = value + rcv[i, d, 5 + part].astype(F32)
            total.append(value)
        gate, up = total
        hid[i, z] = (gate / (1.0 + jnp.exp(-gate)) * up).astype(BF16)
        gather(i, 0, 0).start()
        gather(i, 1, 0).start()

    def arrived_block(i, d, a):
        owner = (z + RING - a - 1) % RING if d == 0 else (z + a + 1) % RING
        block = hid.at[i, owner]
        if a == 3:
            block = block.at[pl.ds(d * HALF, HALF)]
        pltpu.make_async_remote_copy(
            src_ref=block, dst_ref=block,
            send_sem=asend.at[i, d, a], recv_sem=arecv.at[i, d, a],
            device_id=(node, neighbour[d]), device_id_type=MESH,
        ).wait_recv()

    def ag_step(i, a):
        for d in range(2):
            arrived_block(i, d, a - 1)
            gather(i, d, a).start()

    def down(i):
        for d in range(2):
            arrived_block(i, d, 3)
        hidden = jnp.concatenate([hid[i, k] for k in range(RING)], axis=1)
        result = jnp.dot(hidden, wd[...], preferred_element_type=F32).astype(BF16)
        for j in range(PER):
            ret[i * PER + j] = result[j * CAP : (j + 1) * CAP]

        @pl.when(i == 0)
        def _():
            home[0] = result[:CAP]

        @pl.when(i > 0)
        def _():
            giveback(i * PER).start()

        for j in range(1, PER):
            giveback(i * PER + j).start()

    def combine(i):
        @pl.when(i > 0)
        def _():
            giveback(i * PER).wait_recv()

        for j in range(1, PER):
            giveback(i * PER + j).wait_recv()
        rows = home[pl.ds(i * PER, PER)].reshape(R, FEAT)
        weight = comb[:, pl.ds(pl.multiple_of(i * R, R), R)]
        acc[...] += jnp.dot(weight, rows, preferred_element_type=F32)

    def step(i, carry):
        @pl.when(i < C)
        def _():
            @pl.when(i > 0)
            def _():
                dispatch(i * PER).wait_recv()

            for j in range(1, PER):
                dispatch(i * PER + j).wait_recv()
            rs_start(i)

        @pl.when((i >= 1) & (i <= C))
        def _():
            finish_sums(i - 1)

        @pl.when((i >= 2) & (i <= C + 1))
        def _():
            down(i - 2)

        for s in range(1, 4):
            @pl.when(i < C)
            def _():
                rs_step(i, s)

            @pl.when((i >= 1) & (i <= C))
            def _():
                ag_step(i - 1, s)

        @pl.when((i >= 4) & (i <= C + 3))
        def _():
            combine(i - 4)

        return carry

    lax.fori_loop(0, C + 4, step, 0)
    out[...] = acc[...].astype(BF16)

    def drain_nodes(r, carry):
        dispatch(r).wait_send()
        giveback(r).wait_send()
        return carry

    lax.fori_loop(1, NODES, drain_nodes, 0)

    def drain_ring(i, carry):
        for d in range(2):
            for m in range(7):
                partial(i, d, m).wait_send()
            for a in range(4):
                gather(i, d, a).wait_send()
        return carry

    lax.fori_loop(0, C, drain_ring, 0)


def per_device(tokens, w_gate, w_up, w_down, expert_ids, gate_weights):
    select, combine = slot_tables(expert_ids, gate_weights)
    vmem = pl.BlockSpec(memory_space=pltpu.VMEM)
    hbm = pl.BlockSpec(memory_space=pl.ANY)
    dma = pltpu.SemaphoreType.DMA
    return pl.pallas_call(
        kernel,
        out_shape=jax.ShapeDtypeStruct((TOK, FEAT), BF16),
        in_specs=[vmem, vmem, vmem, hbm, hbm, hbm],
        out_specs=vmem,
        scratch_shapes=[
            pltpu.VMEM((FEAT, HID), BF16),
            pltpu.VMEM((FEAT, HID), BF16),
            pltpu.VMEM((HID, FEAT), BF16),
            pltpu.VMEM((NODES, CAP, FEAT), BF16),
            pltpu.VMEM((NODES, CAP, FEAT), BF16),
            pltpu.VMEM((C, 2, 7, R, HS), BF16),
            pltpu.VMEM((C, 2, 7, R, HS), BF16),
            pltpu.VMEM((C, RING, R, HS), BF16),
            pltpu.VMEM((NODES, CAP, FEAT), BF16),
            pltpu.VMEM((NODES, CAP, FEAT), BF16),
            pltpu.VMEM((TOK, FEAT), F32),
            dma((3,)),
            dma((NODES,)), dma((NODES,)),
            dma((NODES,)), dma((NODES,)),
            dma((C, 2, 7)), dma((C, 2, 7)),
            dma((C, 2, 4)), dma((C, 2, 4)),
        ],
        compiler_params=pltpu.CompilerParams(
            collective_id=0, has_side_effects=True, vmem_limit_bytes=56 * 2**20
        ),
    )(select, combine, tokens, w_gate, w_up, w_down)


def solution(mesh):
    placed = (
        P("node", "local"),
        P("node", "local", None),
        P("node", "local", None),
        P("node", None, "local"),
        P("node", None),
        P("node", None),
    )
    return jax.shard_map(
        per_device, mesh=mesh, in_specs=placed, out_specs=P("node", "local"), check_vma=False
    )
```

time: 327 us -> 183 us (0.56)
  waiting for transfers between devices: 198 us -> 0 us
  Pallas kernels: 0 us -> 176 us
  blocking collectives: 53.7 us -> 0 us
  matrix products: 27.2 us -> 0 us
  between operations: 13.5 us -> 0.04 us
  local copies, waits for them, and re-layouts: 14.1 us -> 1.66 us
  starting transfers between devices: 10.5 us -> 0 us
  other arithmetic: 9.15 us -> 5.38 us
    pallas_call x0 -> x1, Pallas kernels: none -> 176 us  [per_device(): pl.pallas_call(kernel, out_shape=jax.ShapeDtypeStruct((TOK, FEAT), BF16),...]
    unnamed x3 -> x0, waiting for transfers between devices: 93.8 us -> none
    all_gather x1 -> x0, waiting for transfers between devices: 58.5 us -> none  [per_device(): lax.all_gather(activated, 'local', axis=0, tiled=True)]
    all_to_all x1 -> x0, blocking collectives: 53.7 us -> none  [per_device(): lax.all_to_all(outbound, 'node', split_axis=0, concat_axis=0, tiled=True)]
    all_to_all x1 -> x0, waiting for transfers between devices: 46 us -> none  [per_device(): lax.all_to_all(returned, 'node', split_axis=0, concat_axis=0, tiled=True)]
    dot_general x5 -> x0, matrix products: 27.2 us -> none  [the longest x1 9.11 us: per_device(): lax.dot_general(lax.all_gather(activated, 'local', axis=0, tiled=True), d...]
    unnamed x8 -> x1, local copies, waits for them, and re-layouts: 13.1 us -> 1.65 us
    all_to_all x1 -> x0, starting transfers between devices: 10.3 us -> none  [per_device(): lax.all_to_all(returned, 'node', split_axis=0, concat_axis=0, tiled=True)]
  transfers between devices with their start and end apart: 3 -> 0, of which waited for: 3 -> 0; matrix products, arithmetic and copies ran while one was open for 0% -> 0% of each run, Pallas kernels for 0% -> 0%
where the time goes in v1:
time: 183 us
  Pallas kernels  176 us (96%)
  other arithmetic  5.38 us (3%)
    pallas_call x1, Pallas kernels, per_device(): pl.pallas_call(kernel, out_shape=jax.ShapeDtypeStruct((TOK, FEAT), BF16),...  176 us

profile of v1, /device:TPU:1, one launch (start us, length us, event | category | flops | bytes accessed | tf_op | source)
XLA Modules:
  0.0 183.0 jit_solution(8864854288978665090)
XLA Ops:
  0.0 0.7 fusion.7
  0.7 0.7 convert_bitcast_fusion
  1.4 0.3 reduce_window_sum.11
  1.8 2.0 %add_convert_fusion.comb = bf16[128,2048]{1,0:T(8,128)(2,1)} fusion(f32[128]{0:T(128)S(1)} %get-tuple-element.22, s32[128]{0:T(128)S(1)} %get-tuple-element.14, f32[128]{0:T(128)S(1)} %get-tuple-element.23, s32[128]{0:T(128)S(1)} %get-tuple-element.15, f32[128]{0:T(128)S(1)} %get-tuple-element.24, s32[128]{0:T(128)S(1)} %get-tuple-element.16, ...), kind=kLoop, calls=%fused_computation | loop fusion | flops 6291456 | bytes 532480 | tf_op jit(solution)/shard_map/convert_element_type | solution.py:54
  3.8 1.6 add_convert_fusion.1.sel
  5.4 175.9 %shard_map.64 = bf16[128,896]{1,0:T(8,128)(2,1)} custom-call(bf16[2048,128]{1,0:T(8,128)(2,1)} %add_convert_fusion.1.sel, bf16[128,2048]{1,0:T(8,128)(2,1)} %add_convert_fusion.comb, bf16[128,896]{1,0:T(8,128)(2,1)} %tok.1, bf16[1,896,1024]{2,1,0:T(8,128)(2,1)} %wg_hbm.1, bf16[1,896,1024]{2,1,0:T(8,128)(2,1)} %wu_hbm.1, bf16[1,1024,896]{2,1,0:T(8,128)(2,1)} %wd_hbm.1), custom_call_target="tpu_custom_call" | custom-call | tf_op jit(solution)/shard_map/pallas_call | solution.py:301
  181.4 1.6 copy.8
  (6 shorter events, 0.1 us)

commit v2 on v0

v2 whole, which is shorter than its diff:
```python
import functools

import jax
import jax.numpy as jnp
from jax import lax
from jax.experimental import pallas as pl
from jax.experimental.pallas import tpu as pltpu
from jax.sharding import PartitionSpec as P

MESH = pl.DeviceIdType.MESH
F32 = jnp.float32
BF16 = jnp.bfloat16

NODES = 32
RING = 8
TOK = 128
FEAT = 896
HID = 1024
HS = HID // RING
CAP = 64

SLOTS = (
    (0, 0, 0), (0, 0, 1),
    (1, 0, 1), (3, 0, 1), (0, 1, 0), (0, 3, 0),
    (0, 1, 1), (0, 3, 1), (2, 0, 0), (2, 0, 1),
    (1, 1, 0), (3, 3, 0), (1, 3, 0), (3, 1, 0),
    (2, 1, 0), (2, 3, 0), (1, 2, 0), (3, 2, 0),
    (0, 2, 0), (0, 2, 1), (2, 2, 0), (2, 2, 1),
    (2, 1, 1), (2, 3, 1), (1, 2, 1), (3, 2, 1),
    (1, 1, 1), (3, 3, 1), (1, 3, 1), (3, 1, 1),
    (1, 0, 0), (3, 0, 0),
)
FULL, PART = 4, 2
C = 2 + (NODES - 2 * PART) // FULL
R = FULL * CAP


def lookup(index, values):
    found = 0
    for k, value in enumerate(values):
        found = found + jnp.where(index == k, value, 0)
    return found


def kernel(
    ids, gates, tok_hbm, wg_hbm, wu_hbm, wd_hbm, out,
    tok, wg, wu, wd, key, dense, outb, arr, snd, rcv, hid, ret, home, acc,
    wsem, dsend, drecv, rsend, rrecv, zsend, zrecv, asend, arecv,
):
    node = lax.axis_index("node")
    z = lax.axis_index("local")
    x, y, core = node // 8, (node // 2) % 4, node % 2
    neighbour = ((z + 1) % RING, (z + RING - 1) % RING)

    pairs = ((tok_hbm, tok), (wg_hbm.at[0], wg), (wu_hbm.at[0], wu), (wd_hbm.at[0], wd))
    loads = [pltpu.make_async_copy(src, dst, wsem.at[k]) for k, (src, dst) in enumerate(pairs)]
    for copy in loads:
        copy.start()

    def partner(r, sign):
        px = (x + sign * lookup(r, [dx for dx, _, _ in SLOTS]) + 4) % 4
        py = (y + sign * lookup(r, [dy for _, dy, _ in SLOTS]) + 4) % 4
        return (px * 4 + py) * 2 + (core + lookup(r, [dc for _, _, dc in SLOTS])) % 2

    barrier = pltpu.get_barrier_semaphore()

    def greet(r, carry):
        pl.semaphore_signal(barrier, inc=1, device_id=(partner(r, 1), z), device_id_type=MESH)
        return carry

    for near in neighbour:
        pl.semaphore_signal(barrier, inc=1, device_id=(node, near), device_id_type=MESH)
    lax.fori_loop(1, NODES, greet, 0)

    expert = ids[...]
    dx = ((expert >> 3) - x) & 3
    dy = (((expert >> 1) & 3) - y) & 3
    dc = ((expert & 1) - core) & 1
    order = [SLOTS.index((k // 8, (k // 2) % 4, k % 2)) for k in range(NODES)]
    slot = lookup(dx * 8 + dy * 2 + dc, order)
    weight = gates[...].astype(F32)
    iota = lax.broadcasted_iota(jnp.int32, (NODES, TOK), 0)
    member = jnp.zeros((NODES, TOK), F32)
    spread = jnp.zeros((NODES, TOK), F32)
    for k in range(ids.shape[0]):
        match = iota == slot[k : k + 1, :]
        member = member + jnp.where(match, 1.0, 0.0)
        spread = spread + jnp.where(match, weight[k : k + 1, :], 0.0)
    lower = lax.broadcasted_iota(jnp.int32, (TOK, TOK), 0) < lax.broadcasted_iota(
        jnp.int32, (TOK, TOK), 1
    )
    before = jnp.dot(
        member.astype(BF16), jnp.where(lower, 1.0, 0.0).astype(BF16), preferred_element_type=F32
    )
    key[...] = jnp.where(member > 0.0, before, -1.0)
    dense[...] = spread

    def base(i):
        return jnp.maximum(FULL * i - (FULL - PART), 0)

    def dispatch(r):
        return pltpu.make_async_remote_copy(
            src_ref=outb.at[r], dst_ref=arr.at[r],
            send_sem=dsend.at[r], recv_sem=drecv.at[r],
            device_id=(partner(r, 1), z), device_id_type=MESH,
        )

    def giveback(r):
        return pltpu.make_async_remote_copy(
            src_ref=ret.at[r], dst_ref=home.at[r],
            send_sem=rsend.at[r], recv_sem=rrecv.at[r],
            device_id=(partner(r, -1), z), device_id_type=MESH,
        )

    def others(i, n, act):
        for j in range(n):
            if j == 0 and n == PART:
                pl.when(i > 0)(functools.partial(act, base(i), 0))
            else:
                act(base(i) + j, j)

    def partial(i, n, d, m):
        rows = pl.ds(0, n * CAP)
        return pltpu.make_async_remote_copy(
            src_ref=snd.at[i, d, m, rows], dst_ref=rcv.at[i, d, m, rows],
            send_sem=zsend.at[i, d, m], recv_sem=zrecv.at[i, d, m],
            device_id=(node, neighbour[d]), device_id_type=MESH,
        )

    def gather(i, n, d, a, back=0):
        far = a + back
        owner = (z + RING - far) % RING if d == 0 else (z + far) % RING
        half = n * CAP // 2
        rows = pl.ds(d * half, half) if a == 3 else pl.ds(0, n * CAP)
        block = hid.at[i, owner, rows]
        return pltpu.make_async_remote_copy(
            src_ref=block, dst_ref=block,
            send_sem=asend.at[i, d, a], recv_sem=arecv.at[i, d, a],
            device_id=(node, neighbour[d]), device_id_type=MESH,
        )

    place = lax.broadcasted_iota(jnp.int32, (CAP, TOK), 0).astype(F32)

    def select(i, n):
        return [place == key[pl.ds(base(i) + j, 1), :] for j in range(n)]

    def pick(i, n):
        onehot = jnp.concatenate([jnp.where(s, 1.0, 0.0) for s in select(i, n)], axis=0)
        rows = jnp.dot(onehot.astype(BF16), tok[...], preferred_element_type=F32).astype(BF16)

        def keep(r, j):
            outb[r] = rows[j * CAP : (j + 1) * CAP]

        others(i, n, keep)
        return rows

    def send_rows(i, n):
        others(i, n, lambda r, j: dispatch(r).start())

    loads[0].wait()
    arr[0] = pick(0, PART)[:CAP]
    pick(1, FULL)
    pl.semaphore_wait(barrier, NODES - 1 + 2)
    send_rows(0, PART)
    send_rows(1, FULL)
    acc[...] = jnp.zeros_like(acc)
    for copy in loads[1:]:
        copy.wait()

    def sums(i, n, to):
        rows = arr[pl.ds(base(i), n)].reshape(n * CAP, FEAT)
        cols = pl.ds(pl.multiple_of(to * HS, HS), HS)
        mat = jnp.concatenate([wg[:, cols], wu[:, cols]], axis=1)
        return jnp.dot(rows, mat, preferred_element_type=F32)

    def at(offset):
        return (z + offset + RING) % RING

    def rs_start(i, n):
        others(i, n, lambda r, j: dispatch(r).wait_recv())
        term = sums(i, n, at(4))
        for d in range(2):
            snd[i, d, 0, : n * CAP] = term[:, d * HS : (d + 1) * HS].astype(BF16)
            partial(i, n, d, 0).start()

    def rs_step(i, n, s):
        terms = (sums(i, n, at(4 - s)), sums(i, n, at(s - 4)))
        for part in range(2):
            for d in range(2):
                term = terms[d][:, part * HS : (part + 1) * HS]
                if s > 1 or part == d:
                    m = 0 if s == 1 else 2 * s - 3 + part
                    partial(i, n, d, m).wait_recv()
                    term = term + rcv[i, d, m, : n * CAP].astype(F32)
                m = 2 * s - 1 + part
                snd[i, d, m, : n * CAP] = term.astype(BF16)
                partial(i, n, d, m).start()

    def finish_sums(i, n):
        term = sums(i, n, z)
        total = []
        for part in range(2):
            value = term[:, part * HS : (part + 1) * HS]
            for d in range(2):
                partial(i, n, d, 5 + part).wait_recv()
                value = value + rcv[i, d, 5 + part, : n * CAP].astype(F32)
            total.append(value)
        gate, up = total
        hid[i, z, : n * CAP] = (gate / (1.0 + jnp.exp(-gate)) * up).astype(BF16)
        for d in range(2):
            gather(i, n, d, 0).start()

    def ag_step(i, n, a):
        for d in range(2):
            gather(i, n, d, a - 1, back=1).wait_recv()
            gather(i, n, d, a).start()

    def down(i, n):
        for d in range(2):
            gather(i, n, d, 3, back=1).wait_recv()
        hidden = jnp.concatenate([hid[i, k, : n * CAP] for k in range(RING)], axis=1)
        result = jnp.dot(hidden, wd[...], preferred_element_type=F32).astype(BF16)

        def send(r, j):
            ret[r] = result[j * CAP : (j + 1) * CAP]
            giveback(r).start()

        others(i, n, send)
        if n == PART:
            @pl.when(i == 0)
            def _():
                home[0] = result[:CAP]

    def combine(i, n):
        others(i, n, lambda r, j: giveback(r).wait_recv())
        rows = home[pl.ds(base(i), n)].reshape(n * CAP, FEAT)
        mix = jnp.concatenate(
            [
                jnp.where(s, dense[pl.ds(base(i) + j, 1), :], 0.0)
                for j, s in enumerate(select(i, n))
            ],
            axis=0,
        )
        acc[...] += lax.dot_general(
            mix.astype(BF16), rows, (((0,), (0,)), ((), ())), preferred_element_type=F32
        )

    def prepare(i, n):
        pick(i, n)
        send_rows(i, n)

    def step(i, carry):
        def live(k, act, *more):
            pl.when((i == k) | (i == C - 1 + k))(lambda: act(i - k, PART, *more))
            pl.when((i > k) & (i < C - 1 + k))(lambda: act(i - k, FULL, *more))

        live(0, rs_start)
        live(1, rs_step, 2)
        live(2, finish_sums)
        live(3, ag_step, 2)
        pl.when(i < C - 3)(lambda: prepare(i + 2, FULL))
        pl.when(i == C - 3)(lambda: prepare(i + 2, PART))
        live(4, down)
        live(0, rs_step, 1)
        live(1, rs_step, 3)
        live(2, ag_step, 1)
        live(3, ag_step, 3)
        live(6, combine)
        return carry

    lax.fori_loop(0, C + 6, step, 0)
    out[...] = acc[...].astype(BF16)

    def drain_nodes(r, carry):
        dispatch(r).wait_send()
        giveback(r).wait_send()
        return carry

    lax.fori_loop(1, NODES, drain_nodes, 0)

    def drain_ring(i, n):
        for d in range(2):
            for m in range(7):
                partial(i, n, d, m).wait_send()
            for a in range(4):
                gather(i, n, d, a).wait_send()

    drain_ring(0, PART)
    drain_ring(C - 1, PART)

    def drain_full(i, carry):
        drain_ring(i, FULL)
        return carry

    lax.fori_loop(1, C - 1, drain_full, 0)


def per_device(tokens, w_gate, w_up, w_down, expert_ids, gate_weights):
    vmem = pl.BlockSpec(memory_space=pltpu.VMEM)
    hbm = pl.BlockSpec(memory_space=pl.ANY)
    dma = pltpu.SemaphoreType.DMA
    return pl.pallas_call(
        kernel,
        out_shape=jax.ShapeDtypeStruct((TOK, FEAT), BF16),
        in_specs=[vmem, vmem, hbm, hbm, hbm, hbm],
        out_specs=vmem,
        scratch_shapes=[
            pltpu.VMEM((TOK, FEAT), BF16),
            pltpu.VMEM((FEAT, HID), BF16),
            pltpu.VMEM((FEAT, HID), BF16),
            pltpu.VMEM((HID, FEAT), BF16),
            pltpu.VMEM((NODES, TOK), F32),
            pltpu.VMEM((NODES, TOK), F32),
            pltpu.VMEM((NODES, CAP, FEAT), BF16),
            pltpu.VMEM((NODES, CAP, FEAT), BF16),
            pltpu.VMEM((C, 2, 7, R, HS), BF16),
            pltpu.VMEM((C, 2, 7, R, HS), BF16),
            pltpu.VMEM((C, RING, R, HS), BF16),
            pltpu.VMEM((NODES, CAP, FEAT), BF16),
            pltpu.VMEM((NODES, CAP, FEAT), BF16),
            pltpu.VMEM((TOK, FEAT), F32),
            dma((4,)),
            dma((NODES,)), dma((NODES,)),
            dma((NODES,)), dma((NODES,)),
            dma((C, 2, 7)), dma((C, 2, 7)),
            dma((C, 2, 4)), dma((C, 2, 4)),
        ],
        compiler_params=pltpu.CompilerParams(
            collective_id=0, has_side_effects=True, vmem_limit_bytes=58 * 2**20
        ),
    )(expert_ids.T, gate_weights.T, tokens, w_gate, w_up, w_down)


def solution(mesh):
    placed = (
        P("node", "local"),
        P("node", "local", None),
        P("node", "local", None),
        P("node", None, "local"),
        P("node", None),
        P("node", None),
    )
    return jax.shard_map(
        per_device, mesh=mesh, in_specs=placed, out_specs=P("node", "local"), check_vma=False
    )
```

time: 327 us -> 161 us (0.49)
  waiting for transfers between devices: 198 us -> 0 us
  Pallas kernels: 0 us -> 159 us
  blocking collectives: 53.7 us -> 0 us
  matrix products: 27.2 us -> 0 us
  between operations: 13.5 us -> 0.01 us
  local copies, waits for them, and re-layouts: 14.1 us -> 1.65 us
  starting transfers between devices: 10.5 us -> 0 us
  other arithmetic: 9.15 us -> 0 us
    pallas_call x0 -> x1, Pallas kernels: none -> 159 us  [per_device(): pl.pallas_call(kernel, out_shape=jax.ShapeDtypeStruct((TOK, FEAT), BF16),...]
    unnamed x3 -> x0, waiting for transfers between devices: 93.8 us -> none
    all_gather x1 -> x0, waiting for transfers between devices: 58.5 us -> none  [per_device(): lax.all_gather(activated, 'local', axis=0, tiled=True)]
    all_to_all x1 -> x0, blocking collectives: 53.7 us -> none  [per_device(): lax.all_to_all(outbound, 'node', split_axis=0, concat_axis=0, tiled=True)]
    all_to_all x1 -> x0, waiting for transfers between devices: 46 us -> none  [per_device(): lax.all_to_all(returned, 'node', split_axis=0, concat_axis=0, tiled=True)]
    dot_general x5 -> x0, matrix products: 27.2 us -> none  [the longest x1 9.11 us: per_device(): lax.dot_general(lax.all_gather(activated, 'local', axis=0, tiled=True), d...]
    unnamed x8 -> x1, local copies, waits for them, and re-layouts: 13.1 us -> 1.65 us
    all_to_all x1 -> x0, starting transfers between devices: 10.3 us -> none  [per_device(): lax.all_to_all(returned, 'node', split_axis=0, concat_axis=0, tiled=True)]
  transfers between devices with their start and end apart: 3 -> 0, of which waited for: 3 -> 0; matrix products, arithmetic and copies ran while one was open for 0% -> 0% of each run, Pallas kernels for 0% -> 0%
where the time goes in v2:
time: 161 us
  Pallas kernels  159 us (99%)
  local copies, waits for them, and re-layouts  1.65 us (1%)
    pallas_call x1, Pallas kernels, per_device(): pl.pallas_call(kernel, out_shape=jax.ShapeDtypeStruct((TOK, FEAT), BF16),...  159 us

profile of v2, /device:TPU:1, one launch (start us, length us, event | category | flops | bytes accessed | tf_op | source)
XLA Modules:
  0.0 161.0 jit_solution(12057628742604545056)
XLA Ops:
  0.0 159.4 %shard_map.64 = bf16[128,896]{1,0:T(8,128)(2,1)} custom-call(s32[8,128]{1,0:T(8,128)} %bitcast.2, bf16[8,128]{1,0:T(8,128)(2,1)} %bitcast.3, bf16[128,896]{1,0:T(8,128)(2,1)} %tok_hbm.1, bf16[1,896,1024]{2,1,0:T(8,128)(2,1)} %wg_hbm.1, bf16[1,896,1024]{2,1,0:T(8,128)(2,1)} %wu_hbm.1, bf16[1,1024,896]{2,1,0:T(8,128)(2,1)} %wd_hbm.1), custom_call_target="tpu_custom_call" | custom-call | tf_op jit(solution)/shard_map/pallas_call | solution.py:302
  159.4 1.6 %copy.8 = bf16[128,896]{1,0:T(8,128)(2,1)} copy(bf16[128,896]{1,0:T(8,128)(2,1)} %shard_map.64) | data formatting | bytes 458752

commit v3 on v2

--- a/solution.py
+++ b/solution.py
@@ -22,12 +22,12 @@
 SLOTS = (
     (0, 0, 0), (0, 0, 1),
     (1, 0, 1), (3, 0, 1), (0, 1, 0), (0, 3, 0),
-    (0, 1, 1), (0, 3, 1), (2, 0, 0), (2, 0, 1),
     (1, 1, 0), (3, 3, 0), (1, 3, 0), (3, 1, 0),
     (2, 1, 0), (2, 3, 0), (1, 2, 0), (3, 2, 0),
     (0, 2, 0), (0, 2, 1), (2, 2, 0), (2, 2, 1),
     (2, 1, 1), (2, 3, 1), (1, 2, 1), (3, 2, 1),
     (1, 1, 1), (3, 3, 1), (1, 3, 1), (3, 1, 1),
+    (0, 1, 1), (0, 3, 1), (2, 0, 0), (2, 0, 1),
     (1, 0, 0), (3, 0, 0),
 )
 FULL, PART = 4, 2
@@ -57,20 +57,24 @@
     for copy in loads:
         copy.start()
 
-    def partner(r, sign):
-        px = (x + sign * lookup(r, [dx for dx, _, _ in SLOTS]) + 4) % 4
-        py = (y + sign * lookup(r, [dy for _, dy, _ in SLOTS]) + 4) % 4
-        return (px * 4 + py) * 2 + (core + lookup(r, [dc for _, _, dc in SLOTS])) % 2
+    def shifted(dx, dy, dc, sign):
+        return (((x + sign * dx + 4) % 4) * 4 + (y + sign * dy + 4) % 4) * 2 + (core + dc) % 2
+
+    def partner(i, n, j, sign):
+        if n == PART:
+            chunks, index = (0, C - 1), jnp.where(i == 0, 0, 1)
+        else:
+            chunks, index = range(1, C - 1), i - 1
+        offsets = [SLOTS[max(FULL * k - (FULL - PART), 0) + j] for k in chunks]
+        return shifted(*(lookup(index, [o[axis] for o in offsets]) for axis in range(3)), sign)
 
     barrier = pltpu.get_barrier_semaphore()
-
-    def greet(r, carry):
-        pl.semaphore_signal(barrier, inc=1, device_id=(partner(r, 1), z), device_id_type=MESH)
-        return carry
 
     for near in neighbour:
         pl.semaphore_signal(barrier, inc=1, device_id=(node, near), device_id_type=MESH)
-    lax.fori_loop(1, NODES, greet, 0)
+    for offset in SLOTS[1:]:
+        other = shifted(*offset, 1)
+        pl.semaphore_signal(barrier, inc=1, device_id=(other, z), device_id_type=MESH)
 
     expert = ids[...]
     dx = ((expert >> 3) - x) & 3
@@ -98,26 +102,28 @@
     def base(i):
         return jnp.maximum(FULL * i - (FULL - PART), 0)
 
-    def dispatch(r):
+    def dispatch(i, n, j):
+        r = base(i) + j
         return pltpu.make_async_remote_copy(
             src_ref=outb.at[r], dst_ref=arr.at[r],
             send_sem=dsend.at[r], recv_sem=drecv.at[r],
-            device_id=(partner(r, 1), z), device_id_type=MESH,
-        )
-
-    def giveback(r):
+            device_id=(partner(i, n, j, 1), z), device_id_type=MESH,
+        )
+
+    def giveback(i, n, j):
+        r = base(i) + j
         return pltpu.make_async_remote_copy(
             src_ref=ret.at[r], dst_ref=home.at[r],
             send_sem=rsend.at[r], recv_sem=rrecv.at[r],
-            device_id=(partner(r, -1), z), device_id_type=MESH,
+            device_id=(partner(i, n, j, -1), z), device_id_type=MESH,
         )
 
     def others(i, n, act):
         for j in range(n):
             if j == 0 and n == PART:
-                pl.when(i > 0)(functools.partial(act, base(i), 0))
+                pl.when(i > 0)(functools.partial(act, 0))
             else:
-                act(base(i) + j, j)
+                act(j)
 
     def partial(i, n, d, m):
         rows = pl.ds(0, n * CAP)
@@ -148,14 +154,14 @@
         onehot = jnp.concatenate([jnp.where(s, 1.0, 0.0) for s in select(i, n)], axis=0)
         rows = jnp.dot(onehot.astype(BF16), tok[...], preferred_element_type=F32).astype(BF16)
 
-        def keep(r, j):
-            outb[r] = rows[j * CAP : (j + 1) * CAP]
+        def keep(j):
+            outb[base(i) + j] = rows[j * CAP : (j + 1) * CAP]
 
         others(i, n, keep)
         return rows
 
     def send_rows(i, n):
-        others(i, n, lambda r, j: dispatch(r).start())
+        others(i, n, lambda j: dispatch(i, n, j).start())
 
     loads[0].wait()
     arr[0] = pick(0, PART)[:CAP]
@@ -177,7 +183,7 @@
         return (z + offset + RING) % RING
 
     def rs_start(i, n):
-        others(i, n, lambda r, j: dispatch(r).wait_recv())
+        others(i, n, lambda j: dispatch(i, n, j).wait_recv())
         term = sums(i, n, at(4))
         for d in range(2):
             snd[i, d, 0, : n * CAP] = term[:, d * HS : (d + 1) * HS].astype(BF16)
@@ -221,9 +227,9 @@
         hidden = jnp.concatenate([hid[i, k, : n * CAP] for k in range(RING)], axis=1)
         result = jnp.dot(hidden, wd[...], preferred_element_type=F32).astype(BF16)
 
-        def send(r, j):
-            ret[r] = result[j * CAP : (j + 1) * CAP]
-            giveback(r).start()
+        def send(j):
+            ret[base(i) + j] = result[j * CAP : (j + 1) * CAP]
+            giveback(i, n, j).start()
 
         others(i, n, send)
         if n == PART:
@@ -231,8 +237,15 @@
             def _():
                 home[0] = result[:CAP]
 
+        others(i, n, lambda j: dispatch(i, n, j).wait_send())
+        for d in range(2):
+            for m in range(7):
+                partial(i, n, d, m).wait_send()
+            for a in range(4):
+                gather(i, n, d, a).wait_send()
+
     def combine(i, n):
-        others(i, n, lambda r, j: giveback(r).wait_recv())
+        others(i, n, lambda j: giveback(i, n, j).wait_recv())
         rows = home[pl.ds(base(i), n)].reshape(n * CAP, FEAT)
         mix = jnp.concatenate(
             [
@@ -244,6 +257,7 @@
         acc[...] += lax.dot_general(
             mix.astype(BF16), rows, (((0,), (0,)), ((), ())), preferred_element_type=F32
         )
+        others(i, n, lambda j: giveback(i, n, j).wait_send())
 
     def prepare(i, n):
         pick(i, n)
@@ -258,41 +272,18 @@
         live(1, rs_step, 2)
         live(2, finish_sums)
         live(3, ag_step, 2)
-        pl.when(i < C - 3)(lambda: prepare(i + 2, FULL))
-        pl.when(i == C - 3)(lambda: prepare(i + 2, PART))
         live(4, down)
         live(0, rs_step, 1)
         live(1, rs_step, 3)
         live(2, ag_step, 1)
         live(3, ag_step, 3)
+        pl.when(i < C - 3)(lambda: prepare(i + 2, FULL))
+        pl.when(i == C - 3)(lambda: prepare(i + 2, PART))
         live(6, combine)
         return carry
 
     lax.fori_loop(0, C + 6, step, 0)
     out[...] = acc[...].astype(BF16)
-
-    def drain_nodes(r, carry):
-        dispatch(r).wait_send()
-        giveback(r).wait_send()
-        return carry
-
-    lax.fori_loop(1, NODES, drain_nodes, 0)
-
-    def drain_ring(i, n):
-        for d in range(2):
-            for m in range(7):
-                partial(i, n, d, m).wait_send()
-            for a in range(4):
-                gather(i, n, d, a).wait_send()
-
-    drain_ring(0, PART)
-    drain_ring(C - 1, PART)
-
-    def drain_full(i, carry):
-        drain_ring(i, FULL)
-        return carry
-
-    lax.fori_loop(1, C - 1, drain_full, 0)
 
 
 def per_device(tokens, w_gate, w_up, w_down, expert_ids, gate_weights):

time: 161 us -> 154 us (0.957)
  Pallas kernels: 159 us -> 152 us
    pallas_call x1, Pallas kernels: 159 us -> 152 us  [per_device(): pl.pallas_call(kernel, out_shape=jax.ShapeDtypeStruct((TOK, FEAT), BF16),...]
where the time goes in v3:
time: 154 us; the launch traced here: 153 us
  Pallas kernels  152 us (99%)
  local copies, waits for them, and re-layouts  1.65 us (1%)
    pallas_call x1, Pallas kernels, per_device(): pl.pallas_call(kernel, out_shape=jax.ShapeDtypeStruct((TOK, FEAT), BF16),...  152 us

profile of v3, /device:TPU:1, one launch (start us, length us, event | category | flops | bytes accessed | tf_op | source)
XLA Modules:
  0.0 153.3 jit_solution(14460440282315951879)
XLA Ops:
  0.0 151.7 %shard_map.64 = bf16[128,896]{1,0:T(8,128)(2,1)} custom-call(s32[8,128]{1,0:T(8,128)} %bitcast.2, bf16[8,128]{1,0:T(8,128)(2,1)} %bitcast.3, bf16[128,896]{1,0:T(8,128)(2,1)} %tok_hbm.1, bf16[1,896,1024]{2,1,0:T(8,128)(2,1)} %wg_hbm.1, bf16[1,896,1024]{2,1,0:T(8,128)(2,1)} %wu_hbm.1, bf16[1,1024,896]{2,1,0:T(8,128)(2,1)} %wd_hbm.1), custom_call_target="tpu_custom_call" | custom-call | tf_op jit(solution)/shard_map/pallas_call | solution.py:293
  151.7 1.6 %copy.8 = bf16[128,896]{1,0:T(8,128)(2,1)} copy(bf16[128,896]{1,0:T(8,128)(2,1)} %shard_map.64) | data formatting | bytes 458752

commit v4 on v3

--- a/solution.py
+++ b/solution.py
@@ -23,11 +23,11 @@
     (0, 0, 0), (0, 0, 1),
     (1, 0, 1), (3, 0, 1), (0, 1, 0), (0, 3, 0),
     (1, 1, 0), (3, 3, 0), (1, 3, 0), (3, 1, 0),
+    (2, 2, 0), (2, 2, 1), (0, 1, 1), (0, 3, 1),
     (2, 1, 0), (2, 3, 0), (1, 2, 0), (3, 2, 0),
-    (0, 2, 0), (0, 2, 1), (2, 2, 0), (2, 2, 1),
     (2, 1, 1), (2, 3, 1), (1, 2, 1), (3, 2, 1),
     (1, 1, 1), (3, 3, 1), (1, 3, 1), (3, 1, 1),
-    (0, 1, 1), (0, 3, 1), (2, 0, 0), (2, 0, 1),
+    (2, 0, 0), (2, 0, 1), (0, 2, 0), (0, 2, 1),
     (1, 0, 0), (3, 0, 0),
 )
 FULL, PART = 4, 2
@@ -237,25 +237,24 @@
             def _():
                 home[0] = result[:CAP]
 
-        others(i, n, lambda j: dispatch(i, n, j).wait_send())
-        for d in range(2):
-            for m in range(7):
-                partial(i, n, d, m).wait_send()
-            for a in range(4):
-                gather(i, n, d, a).wait_send()
-
     def combine(i, n):
-        others(i, n, lambda j: giveback(i, n, j).wait_recv())
-        rows = home[pl.ds(base(i), n)].reshape(n * CAP, FEAT)
         mix = jnp.concatenate(
             [
                 jnp.where(s, dense[pl.ds(base(i) + j, 1), :], 0.0)
                 for j, s in enumerate(select(i, n))
             ],
             axis=0,
-        )
+        ).astype(BF16)
+        others(i, n, lambda j: dispatch(i, n, j).wait_send())
+        for d in range(2):
+            for m in range(7):
+                partial(i, n, d, m).wait_send()
+            for a in range(4):
+                gather(i, n, d, a).wait_send()
+        others(i, n, lambda j: giveback(i, n, j).wait_recv())
+        rows = home[pl.ds(base(i), n)].reshape(n * CAP, FEAT)
         acc[...] += lax.dot_general(
-            mix.astype(BF16), rows, (((0,), (0,)), ((), ())), preferred_element_type=F32
+            mix, rows, (((0,), (0,)), ((), ())), preferred_element_type=F32
         )
         others(i, n, lambda j: giveback(i, n, j).wait_send())
 

time: 154 us -> 154 us (level)
  no operation moved by 1% of the time
where the time goes in v4:
time: 154 us; the launch traced here: 153 us
  Pallas kernels  152 us (99%)
  local copies, waits for them, and re-layouts  1.65 us (1%)
    pallas_call x1, Pallas kernels, per_device(): pl.pallas_call(kernel, out_shape=jax.ShapeDtypeStruct((TOK, FEAT), BF16),...  152 us

profile of v4, /device:TPU:1, one launch (start us, length us, event | category | flops | bytes accessed | tf_op | source)
XLA Modules:
  0.0 153.4 jit_solution(10474323402612430458)
XLA Ops:
  0.0 151.8 %shard_map.64 = bf16[128,896]{1,0:T(8,128)(2,1)} custom-call(s32[8,128]{1,0:T(8,128)} %bitcast.2, bf16[8,128]{1,0:T(8,128)(2,1)} %bitcast.3, bf16[128,896]{1,0:T(8,128)(2,1)} %tok_hbm.1, bf16[1,896,1024]{2,1,0:T(8,128)(2,1)} %wg_hbm.1, bf16[1,896,1024]{2,1,0:T(8,128)(2,1)} %wu_hbm.1, bf16[1,1024,896]{2,1,0:T(8,128)(2,1)} %wd_hbm.1), custom_call_target="tpu_custom_call" | custom-call | tf_op jit(solution)/shard_map/pallas_call | solution.py:292
  151.8 1.6 %copy.8 = bf16[128,896]{1,0:T(8,128)(2,1)} copy(bf16[128,896]{1,0:T(8,128)(2,1)} %shard_map.64) | data formatting | bytes 458752

commit v5 on v4

--- a/solution.py
+++ b/solution.py
@@ -50,7 +50,12 @@
     node = lax.axis_index("node")
     z = lax.axis_index("local")
     x, y, core = node // 8, (node // 2) % 4, node % 2
-    neighbour = ((z + 1) % RING, (z + RING - 1) % RING)
+    turn = 1 - 2 * core
+
+    def at(offset):
+        return (z + turn * offset + RING) % RING
+
+    neighbour = (at(1), at(-1))
 
     pairs = ((tok_hbm, tok), (wg_hbm.at[0], wg), (wu_hbm.at[0], wu), (wd_hbm.at[0], wd))
     loads = [pltpu.make_async_copy(src, dst, wsem.at[k]) for k, (src, dst) in enumerate(pairs)]
@@ -135,7 +140,7 @@
 
     def gather(i, n, d, a, back=0):
         far = a + back
-        owner = (z + RING - far) % RING if d == 0 else (z + far) % RING
+        owner = at(-far if d == 0 else far)
         half = n * CAP // 2
         rows = pl.ds(d * half, half) if a == 3 else pl.ds(0, n * CAP)
         block = hid.at[i, owner, rows]
@@ -178,9 +183,6 @@
         cols = pl.ds(pl.multiple_of(to * HS, HS), HS)
         mat = jnp.concatenate([wg[:, cols], wu[:, cols]], axis=1)
         return jnp.dot(rows, mat, preferred_element_type=F32)
-
-    def at(offset):
-        return (z + offset + RING) % RING
 
     def rs_start(i, n):
         others(i, n, lambda j: dispatch(i, n, j).wait_recv())
@@ -222,10 +224,16 @@
             gather(i, n, d, a).start()
 
     def down(i, n):
+        def product(offsets):
+            owners = [at(o) for o in offsets]
+            hidden = jnp.concatenate([hid[i, k, : n * CAP] for k in owners], axis=1)
+            rows = [wd[pl.ds(pl.multiple_of(k * HS, HS), HS), :] for k in owners]
+            return jnp.dot(hidden, jnp.concatenate(rows, axis=0), preferred_element_type=F32)
+
+        near = product((0, 1, -1, 2, -2, 3, -3))
         for d in range(2):
             gather(i, n, d, 3, back=1).wait_recv()
-        hidden = jnp.concatenate([hid[i, k, : n * CAP] for k in range(RING)], axis=1)
-        result = jnp.dot(hidden, wd[...], preferred_element_type=F32).astype(BF16)
+        result = (near + product((4,))).astype(BF16)
 
         def send(j):
             ret[base(i) + j] = result[j * CAP : (j + 1) * CAP]

time: 154 us -> 154 us (level)
  no operation moved by 1% of the time
where the time goes in v5:
time: 154 us
  Pallas kernels  152 us (99%)
  local copies, waits for them, and re-layouts  1.65 us (1%)
    pallas_call x1, Pallas kernels, per_device(): pl.pallas_call(kernel, out_shape=jax.ShapeDtypeStruct((TOK, FEAT), BF16),...  152 us

profile of v5, /device:TPU:1, one launch (start us, length us, event | category | flops | bytes accessed | tf_op | source)
XLA Modules:
  0.0 153.6 jit_solution(5080659856251682025)
XLA Ops:
  0.0 152.0 %shard_map.64 = bf16[128,896]{1,0:T(8,128)(2,1)} custom-call(s32[8,128]{1,0:T(8,128)} %bitcast.2, bf16[8,128]{1,0:T(8,128)(2,1)} %bitcast.3, bf16[128,896]{1,0:T(8,128)(2,1)} %tok_hbm.1, bf16[1,896,1024]{2,1,0:T(8,128)(2,1)} %wg_hbm.1, bf16[1,896,1024]{2,1,0:T(8,128)(2,1)} %wu_hbm.1, bf16[1,1024,896]{2,1,0:T(8,128)(2,1)} %wd_hbm.1), custom_call_target="tpu_custom_call" | custom-call | tf_op jit(solution)/shard_map/pallas_call | solution.py:300
  152.0 1.6 %copy.8 = bf16[128,896]{1,0:T(8,128)(2,1)} copy(bf16[128,896]{1,0:T(8,128)(2,1)} %shard_map.64) | data formatting | bytes 458752
